TPU v7x, 256 devices: a whole 4x4x8 slice. The times are simulated.
256 devices in a mesh: slab: 64 (over z, y, core), tile: 4 (over x).
Axes of the slice: x: 4, y: 4, z: 8, core: 2. Of those that a mesh axis runs over, the one named last changes fastest.
Arguments:
- snapshots: bfloat16 [8192, 128, 256], P(('slab', 'tile')), may hold values from -1210 to 1210
- routes: int32 [8192, 1], P(('slab', 'tile')), may hold values from 0 to 3; in each aligned block of 32 rows (0 to 31, 32 to 63, ...) at most 10 rows name the same one
- sketch_matrix: bfloat16 [256, 128], replicated, may hold values from -0.375 to 0.375
Outputs:
- basis_rows: bfloat16 [10240, 128, 128], P(('slab', 'tile'))
- triangle: float32 [128, 128], replicated
Inputs may be any that keep to these rules, and one draw needn't show every extreme that they name: `routes`: among the 32 blocks of one device no owner value appears more than 10 times; a block with value o goes to tile o of its own slab.
All inputs are finite; a program needn't handle non-finite values.
Results may differ from a plain program's by a relative error of at most 0.0065.
Values may be sent and summed in bfloat16 or wider, within the bound.
A program may use at most 64 MiB of HBM per device.

v0:
```python
import math
import jax
import jax.numpy as jnp
from jax import lax
from jax.sharding import PartitionSpec as P

SEND = 10


def slot_selector(routes, tiles, slots):
    destination = routes[:, 0]
    owners = jnp.arange(tiles, dtype=jnp.int32)
    owner_hit = (destination[None, :] == owners[:, None]).astype(jnp.int32)
    earlier = jnp.cumsum(owner_hit, axis=1) - owner_hit
    slot_ids = jnp.arange(slots, dtype=jnp.int32)
    chosen = owner_hit[:, None, :] * (earlier[:, None, :] == slot_ids[None, :, None]).astype(
        jnp.int32
    )
    return chosen.reshape(tiles * slots, routes.shape[0]).astype(jnp.bfloat16)


def place_blocks(selector, block_data):
    block_count, cell_rows, width = block_data.shape
    flattened = jnp.dot(
        selector,
        block_data.reshape(block_count, cell_rows * width),
        preferred_element_type=jnp.float32,
    )
    return flattened.astype(jnp.bfloat16).reshape(selector.shape[0], cell_rows, width)


def global_factor(partial_gram):
    gram_matrix = lax.psum(partial_gram, ("slab", "tile"))
    return jnp.linalg.cholesky(gram_matrix)


def local(snapshots, routes, sketch_matrix):
    n_tile = lax.axis_size("tile")
    n_slab = lax.axis_size("slab")
    block_count, cell_rows, snap_width = snapshots.shape
    sketch_width = sketch_matrix.shape[1]
    cell_root = math.sqrt(block_count * cell_rows * n_slab * n_tile)
    selector = slot_selector(routes, n_tile, SEND)
    outgoing = place_blocks(selector, snapshots).reshape(n_tile, SEND, cell_rows, snap_width)
    product = jnp.einsum(
        "tjrc,cd->tjrd",
        lax.all_to_all(outgoing, "tile", split_axis=0, concat_axis=0, tiled=True),
        sketch_matrix,
        preferred_element_type=jnp.float32,
    )
    sketch = product.astype(jnp.bfloat16)
    sketch_rows = sketch.reshape(-1, sketch_width)
    partial_gram = lax.dot_general(
        sketch_rows, sketch_rows, (((0,), (0,)), ((), ())), preferred_element_type=jnp.float32
    )
    lower_factor = global_factor(partial_gram)
    identity = jnp.eye(sketch_width, dtype=jnp.float32)
    inverse_factor = jax.scipy.linalg.solve_triangular(lower_factor, identity, lower=True)
    wide_rows = sketch_rows.astype(jnp.float32)
    scaled = (
        jnp.dot(wide_rows, inverse_factor.T, precision=lax.Precision.HIGHEST) * cell_root
    ).astype(jnp.bfloat16)
    basis_rows = scaled.reshape(n_tile * SEND, cell_rows, sketch_width)
    return (basis_rows, lower_factor.T / cell_root)


def solution(mesh):
    return jax.shard_map(
        local,
        mesh=mesh,
        in_specs=(P(("slab", "tile"), None, None), P(("slab", "tile"), None), P()),
        out_specs=(P(("slab", "tile"), None, None), P()),
        check_vma=False,
    )
```

profile of v0, /device:TPU:1, one launch (start us, length us, event | category | flops | bytes accessed | tf_op | source)
XLA Modules:
  0.0 325.9 jit_solution(3418719268438397038)
XLA Ops:
  7.2 0.0 copy-start
  7.2 0.0 all-reduce.2.cloned.1.call-start
  7.2 0.7 fusion.5
  7.9 0.2 reduce_window_sum.11
  8.1 0.7 fusion.6
  8.8 2.8 copy.17
  11.6 0.8 convolution_convert_fusion
  12.4 0.6 copy.18
  13.0 35.5 %all_to_all.5 = bf16[4,10,128,256]{3,2,1,0:T(8,128)(2,1)S(1)} all-to-all(bf16[4,10,128,256]{3,2,1,0:T(8,128)(2,1)S(1)} %bitcast.35), channel_id=1, replica_groups=mesh['slab'=64,'tile'=4] {'tile'}, dimensions={0} | all-to-all | bytes 5242880 | tf_op jit(solution)/shard_map/all_to_all | solution.py:47
  48.6 0.0 copy-done
  48.6 0.8 convolution_convert_fusion.1
  49.4 1.2 convolution_bitcast_fusion
  50.6 0.0 all-reduce.2.cloned.1.call-update
  50.6 240.6 %all-reduce.2.cloned.1.call-done = f32[128,128]{0,1:T(8,128)} async-done(((f32[128,128]{0,1:T(8,128)}), f32[128,128]{0,1:T(8,128)}) %all-reduce.2.cloned.1.call-update) | async-done | bytes 65552 | tf_op jit(solution)/shard_map/psum | solution.py:33
  291.2 0.9 copy.11
  292.1 0.9 fusion.4
  293.0 11.7 %cholesky.17 = f32[128,128]{1,0:T(8,128)S(1)} custom-call(f32[128,128]{1,0:T(8,128)S(1)} %fusion.4), custom_call_target="Cholesky" | custom-call | tf_op jit(solution)/shard_map/jit(cholesky)/cholesky | solution.py:34
  304.7 0.6 compare_reduce_fusion
  305.4 0.7 multiply_bitcast_fusion
  306.0 0.7 copy.12
  306.8 9.8 %custom-call.7 = f32[1,128,128]{1,2,0:T(8,128)S(1)} custom-call(f32[1,128,128]{2,1,0:T(8,128)S(1)} %get-tuple-element.7), custom_call_target="InvertDiagBlocksLowerTriangular" | custom-call | tf_op jit(solution)/shard_map/jit(_solve_triangular)/triangular_solve | solution.py:58
  316.6 0.2 fusion.2
  316.8 2.3 fusion
  (3 shorter events, 0.1 us)
Async XLA Ops:
  7.2 41.4 %copy-start = (bf16[256,128]{1,0:T(8,128)(2,1)S(1)}, bf16[256,128]{1,0:T(8,128)(2,1)}, u32[]{:S(2)}) copy-start(bf16[256,128]{1,0:T(8,128)(2,1)} %param.5) | copy-start | bytes 196612
  7.2 284.0 %all-reduce.2.cloned.1.call-start = ((), (), s32[]{:S(2)}) async-start(), calls=%async_computation.1 | async-start | bytes 131072 | tf_op jit(solution)/shard_map/psum | solution.py:33
Sparse Core Ops, SparseCore 0:
  50.7 240.4 all-reduce.1
where the time goes:
time: 326 us
  waiting for transfers between devices  241 us (74%)
  blocking collectives  35.5 us (11%)
  other arithmetic  25.2 us (8%)
  between operations  14.1 us (4%)
  matrix products  5.37 us (2%)
  local copies, waits for them, and re-layouts  5.09 us (2%)
    psum x1, waiting for transfers between devices, global_factor(): gram_matrix = lax.psum(partial_gram, ('slab', 'tile'))  241 us
    all_to_all x1, blocking collectives, local(): lax.all_to_all(outgoing, 'tile', split_axis=0, concat_axis=0, tiled=True)  35.5 us
    another operation x3, other arithmetic, global_factor(): return jnp.linalg.cholesky(gram_matrix)  12.4 us
    another operation x1, other arithmetic, local(): jax.scipy.linalg.solve_triangular(lower_factor, identity, lower=True)  9.81 us
  transfers between devices with their start and end apart: 1, of which 1 were waited for; matrix products, arithmetic and copies ran while one was open for 0% of the time, Pallas kernels for 0%

commit v1 on v0

--- a/solution.py
+++ b/solution.py
@@ -30,7 +30,9 @@
 
 
 def global_factor(partial_gram):
-    gram_matrix = lax.psum(partial_gram, ("slab", "tile"))
+    gram_matrix = partial_gram
+    for axis in ("slab", "tile"):
+        gram_matrix = lax.psum(gram_matrix, axis)
     return jnp.linalg.cholesky(gram_matrix)
 
 

time: 326 us -> 300 us (0.920)
  waiting for transfers between devices: 241 us -> 213 us
    psum x1 -> x2, waiting for transfers between devices: 241 us -> 213 us  [global_factor(): gram_matrix = lax.psum(gram_matrix, axis)]
  transfers between devices with their start and end apart: 1 -> 2, of which waited for: 1 -> 2; matrix products, arithmetic and copies ran while one was open for 0% -> 0% of each run, Pallas kernels for 0% -> 0%
where the time goes in v1:
time: 300 us; the launch traced here: 299 us
  waiting for transfers between devices  213 us (71%)
  blocking collectives  35.5 us (12%)
  other arithmetic  25.2 us (8%)
  between operations  14.1 us (5%)
  matrix products  5.37 us (2%)
  local copies, waits for them, and re-layouts  5.09 us (2%)
    psum x2, waiting for transfers between devices, global_factor(): gram_matrix = lax.psum(gram_matrix, axis)  213 us
    all_to_all x1, blocking collectives, local(): lax.all_to_all(outgoing, 'tile', split_axis=0, concat_axis=0, tiled=True)  35.5 us
    another operation x3, other arithmetic, global_factor(): return jnp.linalg.cholesky(gram_matrix)  12.4 us
    another operation x1, other arithmetic, local(): jax.scipy.linalg.solve_triangular(lower_factor, identity, lower=True)  9.81 us
  transfers between devices with their start and end apart: 2, of which 2 were waited for; matrix products, arithmetic and copies ran while one was open for 0% of the time, Pallas kernels for 0%

profile of v1, /device:TPU:1, one launch (start us, length us, event | category | flops | bytes accessed | tf_op | source)
XLA Modules:
  0.0 298.8 jit_solution(3033724374802596473)
XLA Ops:
  7.2 0.0 copy-start
  7.2 0.0 all-reduce.3.cloned.1.call-start
  7.2 0.7 fusion.5
  7.9 0.2 reduce_window_sum.11
  8.1 0.7 fusion.6
  8.8 2.8 copy.17
  11.6 0.8 convolution_convert_fusion
  12.4 0.6 copy.18
  13.0 35.5 %all_to_all.5 = bf16[4,10,128,256]{3,2,1,0:T(8,128)(2,1)S(1)} all-to-all(bf16[4,10,128,256]{3,2,1,0:T(8,128)(2,1)S(1)} %bitcast.35), channel_id=1, replica_groups=mesh['slab'=64,'tile'=4] {'tile'}, dimensions={0} | all-to-all | bytes 5242880 | tf_op jit(solution)/shard_map/all_to_all | solution.py:49
  48.6 0.0 copy-done
  48.6 0.8 convolution_convert_fusion.1
  49.4 1.2 convolution_bitcast_fusion
  50.6 0.0 all-reduce.3.cloned.1.call-update
  50.6 0.0 all-reduce.5.cloned.1.call-start
  50.7 170.3 %all-reduce.3.cloned.1.call-done = f32[128,128]{0,1:T(8,128)} async-done(((f32[128,128]{0,1:T(8,128)}), f32[128,128]{0,1:T(8,128)}) %all-reduce.3.cloned.1.call-update) | async-done | bytes 65552 | tf_op jit(solution)/shard_map/psum | solution.py:35
  221.0 0.0 all-reduce.5.cloned.1.call-update
  221.0 43.1 %all-reduce.5.cloned.1.call-done = f32[128,128]{0,1:T(8,128)} async-done(((f32[128,128]{0,1:T(8,128)}), f32[128,128]{0,1:T(8,128)}) %all-reduce.5.cloned.1.call-update) | async-done | bytes 65552 | tf_op jit(solution)/shard_map/psum | solution.py:35
  264.1 0.9 copy.11
  265.0 0.9 fusion.4
  265.9 11.7 %cholesky.17 = f32[128,128]{1,0:T(8,128)S(1)} custom-call(f32[128,128]{1,0:T(8,128)S(1)} %fusion.4), custom_call_target="Cholesky" | custom-call | tf_op jit(solution)/shard_map/jit(cholesky)/cholesky | solution.py:36
  277.6 0.6 compare_reduce_fusion
  278.3 0.7 multiply_bitcast_fusion
  278.9 0.7 copy.12
  279.7 9.8 %custom-call.7 = f32[1,128,128]{1,2,0:T(8,128)S(1)} custom-call(f32[1,128,128]{2,1,0:T(8,128)S(1)} %get-tuple-element.7), custom_call_target="InvertDiagBlocksLowerTriangular" | custom-call | tf_op jit(solution)/shard_map/jit(_solve_triangular)/triangular_solve | solution.py:60
  289.5 0.2 fusion.2
  289.7 2.3 fusion
  (3 shorter events, 0.1 us)
Async XLA Ops:
  7.2 41.4 %copy-start = (bf16[256,128]{1,0:T(8,128)(2,1)S(1)}, bf16[256,128]{1,0:T(8,128)(2,1)}, u32[]{:S(2)}) copy-start(bf16[256,128]{1,0:T(8,128)(2,1)} %param.5) | copy-start | bytes 196612
  7.2 213.8 %all-reduce.3.cloned.1.call-start = ((), (), s32[]{:S(2)}) async-start(), calls=%async_computation.1 | async-start | bytes 131072 | tf_op jit(solution)/shard_map/psum | solution.py:35
  50.6 213.5 %all-reduce.5.cloned.1.call-start = ((), (), s32[]{:S(2)}) async-start(), calls=%async_computation.2 | async-start | bytes 131072 | tf_op jit(solution)/shard_map/psum | solution.py:35
Sparse Core Ops, SparseCore 0:
  50.7 170.2 all-reduce.2
  223.3 40.7 all-reduce.4
